TPU v7x, 128 devices: a whole 4x4x4 slice. The times are simulated.
128 devices in a mesh: depth: 4 (over z_hi, core), row: 8 (over x, z_lo), col: 4 (over y).
Axes of the slice: x: 4, y: 4, z: 4 (z_hi: 2, z_lo: 2; z = z_hi * 2 + z_lo), core: 2. Of those that a mesh axis runs over, the one named last changes fastest.
Arguments:
- tokens_in: bfloat16 [4096, 4096], P(('depth', 'row'), 'col'), may hold values from -6 to 6
- grad_out: bfloat16 [4096, 4096], P(('depth', 'row'), 'col'), may hold values from -6 to 6
- gate_pre: bfloat16 [4096, 14336], P(('depth', 'col'), 'row'), may hold values from -6 to 6
- up_pre: bfloat16 [4096, 14336], P(('depth', 'col'), 'row'), may hold values from -6 to 6
- gate_weight: bfloat16 [4096, 14336], P(('col', 'depth'), 'row'), may hold values from -0.09375 to 0.09375
- up_weight: bfloat16 [4096, 14336], P(('col', 'depth'), 'row'), may hold values from -0.09375 to 0.09375
- down_weight: bfloat16 [14336, 4096], P('row', ('col', 'depth')), may hold values from -0.046875 to 0.046875
Outputs:
- grad_in: bfloat16 [4096, 4096], P(('depth', 'row'), 'col')
- grad_gate_w: bfloat16 [4096, 14336], P(('col', 'depth'), 'row')
- grad_up_w: bfloat16 [4096, 14336], P(('col', 'depth'), 'row')
- grad_down_w: bfloat16 [14336, 4096], P('row', ('col', 'depth'))
All inputs are finite; a program needn't handle non-finite values.
Results may differ from a plain program's by a relative error of at most 0.025.
Values may be sent and summed in bfloat16 or wider, within the bound.
A program may use at most 128 MiB of HBM per device.

v0:
```python
import math

import jax
import jax.numpy as jnp
from jax import lax
from jax.sharding import PartitionSpec as P


def backward_gates(hidden_grad, gate_pre, up_pre):
    gate_value = gate_pre.astype(jnp.float32)
    up_value = up_pre.astype(jnp.float32)
    sigmoid = jax.nn.sigmoid(gate_value)
    swish_value = gate_value * sigmoid
    grad_gate = (hidden_grad * up_value * sigmoid * (1.0 + gate_value * (1.0 - sigmoid))).astype(
        jnp.bfloat16
    )
    grad_up = (hidden_grad * swish_value).astype(jnp.bfloat16)
    activ = (swish_value * up_value).astype(jnp.bfloat16)
    return (grad_gate, grad_up, activ)


def contract_last(left, right):
    return lax.dot_general(
        left, right, (((1,), (1,)), ((), ())), preferred_element_type=jnp.float32
    )


def contract_first(left, right):
    return lax.dot_general(
        left, right, (((0,), (0,)), ((), ())), preferred_element_type=jnp.float32
    )


def shards(tokens_in, grad_out, gate_pre, up_pre, gate_weight, up_weight, down_weight):
    token_whole, grad_whole = (
        lax.all_gather(tokens_in, "row", axis=0, tiled=True),
        lax.all_gather(grad_out, "row", axis=0, tiled=True),
    )
    down_whole = lax.all_gather(down_weight, "depth", axis=1, tiled=True)
    hidden_grad = lax.psum_scatter(
        contract_last(grad_whole, down_whole).astype(jnp.bfloat16),
        "col",
        scatter_dimension=0,
        tiled=True,
    ).astype(jnp.float32)
    grad_gate, grad_up, activ = backward_gates(hidden_grad, gate_pre, up_pre)
    gate_whole, up_whole, activ_whole = (
        lax.all_gather(grad_gate, "col", axis=0, tiled=True),
        lax.all_gather(grad_up, "col", axis=0, tiled=True),
        lax.all_gather(activ, "col", axis=0, tiled=True),
    )
    token_count = token_whole.shape[0] * lax.axis_size("depth")
    grad_scale = 1.0 / math.sqrt(token_count)
    partial_in = contract_last(gate_whole, lax.all_gather(gate_weight, "depth", axis=0, tiled=True))
    partial_in = partial_in + contract_last(
        up_whole, lax.all_gather(up_weight, "depth", axis=0, tiled=True)
    )
    token_cols = token_whole
    gate_sums = lax.psum_scatter(
        contract_first(token_cols, gate_whole).astype(jnp.bfloat16),
        "depth",
        scatter_dimension=0,
        tiled=True,
    ).astype(jnp.float32)
    token_cols = token_whole
    up_sums = lax.psum_scatter(
        contract_first(token_cols, up_whole).astype(jnp.bfloat16),
        "depth",
        scatter_dimension=0,
        tiled=True,
    ).astype(jnp.float32)
    grad_in = lax.psum_scatter(
        partial_in.astype(jnp.bfloat16), "row", scatter_dimension=0, tiled=True
    )
    down_term = contract_first(activ_whole, grad_whole)
    down_sums = lax.psum_scatter(
        down_term.astype(jnp.bfloat16), "depth", scatter_dimension=1, tiled=True
    ).astype(jnp.float32)
    return (
        grad_in,
        (gate_sums * grad_scale).astype(jnp.bfloat16),
        (up_sums * grad_scale).astype(jnp.bfloat16),
        (down_sums * grad_scale).astype(jnp.bfloat16),
    )


def solution(mesh):
    return jax.shard_map(
        shards,
        mesh=mesh,
        in_specs=(
            P(("depth", "row"), "col"),
            P(("depth", "row"), "col"),
            P(("depth", "col"), "row"),
            P(("depth", "col"), "row"),
            P(("col", "depth"), "row"),
            P(("col", "depth"), "row"),
            P("row", ("col", "depth")),
        ),
        out_specs=(
            P(("depth", "row"), "col"),
            P(("col", "depth"), "row"),
            P(("col", "depth"), "row"),
            P("row", ("col", "depth")),
        ),
        check_vma=False,
    )
```

profile of v0, /device:TPU:32, one launch (start us, length us, event | category | flops | bytes accessed | tf_op | source)
XLA Modules:
  0.0 627.6 jit_solution(12764110676294560932)
XLA Ops:
  8.7 54.0 %all-gather.9.cloned.1.call-done = bf16[1024,1024]{1,0:T(8,128)(2,1)} async-done(((bf16[128,1024]{1,0:T(8,128)(2,1)}), bf16[1024,1024]{1,0:T(8,128)(2,1)}) %all-gather.9.cloned.1.call-update) | async-done | bytes 2097168 | tf_op jit(solution)/shard_map/all_gather | solution.py:37
  62.7 37.4 %all-gather.11.cloned.1.call-done = bf16[1792,1024]{1,0:T(8,128)(2,1)} async-done(((bf16[1792,256]{1,0:T(8,128)(2,1)}), bf16[1792,1024]{1,0:T(8,128)(2,1)}) %all-gather.11.cloned.1.call-update) | async-done | bytes 3670032 | tf_op jit(solution)/shard_map/all_gather | solution.py:39
  100.1 8.4 %convolution_convert_fusion.3 = bf16[1024,1792]{1,0:T(8,128)(2,1)} fusion(bf16[1024,1024]{1,0:T(8,128)(2,1)} %all-gather.9.cloned.1.call-done, bf16[1792,1024]{1,0:T(8,128)(2,1)} %all-gather.11.cloned.1.call-done), kind=kOutput, calls=%fused_computation.4 | convolution fusion | flops 3759931392 | bytes 9437184 | tf_op jit(solution)/shard_map/dot_general | solution.py:23
  109.2 42.2 %reduce-scatter.6.cloned.1.call-done = bf16[256,1792]{1,0:T(8,128)(2,1)} async-done(((bf16[1024,1792]{1,0:T(8,128)(2,1)}), bf16[256,1792]{1,0:T(8,128)(2,1)}) %reduce-scatter.6.cloned.1.call-update) | async-done | bytes 917520 | tf_op jit(solution)/shard_map/reduce_scatter | solution.py:40
  151.3 3.7 fusion.6
  158.0 45.6 %all-gather.21.cloned.1.call-done = bf16[1024,1024]{1,0:T(8,128)(2,1)} async-done(((bf16[128,1024]{1,0:T(8,128)(2,1)}), bf16[1024,1024]{1,0:T(8,128)(2,1)}) %all-gather.21.cloned.1.call-update) | async-done | bytes 2097168 | tf_op jit(solution)/shard_map/all_gather | solution.py:36
  203.6 46.4 %all-gather.13.cloned.1.call-done = bf16[1024,1792]{1,0:T(8,128)(2,1)} async-done(((bf16[256,1792]{1,0:T(8,128)(2,1)}), bf16[1024,1792]{1,0:T(8,128)(2,1)}) %all-gather.13.cloned.1.call-update) | async-done | bytes 3670032 | tf_op jit(solution)/shard_map/all_gather | solution.py:48
  250.1 8.6 %fusion = bf16[1024,1792]{0,1:T(8,128)(2,1)} fusion(bf16[1024,1792]{1,0:T(8,128)(2,1)} %all-gather.13.cloned.1.call-done, bf16[1024,1024]{1,0:T(8,128)(2,1)} %all-gather.21.cloned.1.call-done), kind=kOutput, calls=%fused_computation.5 | convolution fusion | flops 3759931392 | bytes 9437184 | tf_op jit(solution)/shard_map/dot_general | solution.py:29
  258.7 37.6 %all-gather.17.cloned.1.call-done = bf16[1024,1792]{1,0:T(8,128)(2,1)} async-done(((bf16[256,1792]{1,0:T(8,128)(2,1)}), bf16[1024,1792]{1,0:T(8,128)(2,1)}) %all-gather.17.cloned.1.call-update) | async-done | bytes 3670032 | tf_op jit(solution)/shard_map/all_gather | solution.py:49
  296.4 7.6 %fusion.1 = bf16[1024,1792]{0,1:T(8,128)(2,1)} fusion(bf16[1024,1792]{1,0:T(8,128)(2,1)} %all-gather.17.cloned.1.call-done, bf16[1024,1024]{1,0:T(8,128)(2,1)S(1)} %copy-done.3), kind=kOutput, calls=%fused_computation.6 | convolution fusion | flops 3759931392 | bytes 9437184 | tf_op jit(solution)/shard_map/dot_general | solution.py:29
  304.2 38.6 %all-gather.23.cloned.1.call-done = bf16[1024,1792]{1,0:T(8,128)(2,1)} async-done(((bf16[256,1792]{1,0:T(8,128)(2,1)}), bf16[1024,1792]{1,0:T(8,128)(2,1)}) %all-gather.23.cloned.1.call-update) | async-done | bytes 3670032 | tf_op jit(solution)/shard_map/all_gather | solution.py:50
  342.8 7.6 %convolution_convert_fusion = bf16[1792,1024]{1,0:T(8,128)(2,1)} fusion(bf16[1024,1792]{1,0:T(8,128)(2,1)} %all-gather.23.cloned.1.call-done, bf16[1024,1024]{1,0:T(8,128)(2,1)S(1)} %copy-done.2), kind=kOutput, calls=%fused_computation.1 | convolution fusion | flops 3759931392 | bytes 9437184 | tf_op jit(solution)/shard_map/dot_general | solution.py:29
  350.4 29.1 %all-gather.15.cloned.1.call-done = bf16[1024,1792]{1,0:T(8,128)(2,1)} async-done(((bf16[256,1792]{1,0:T(8,128)(2,1)}), bf16[1024,1792]{1,0:T(8,128)(2,1)}) %all-gather.15.cloned.1.call-update) | async-done | bytes 3670032 | tf_op jit(solution)/shard_map/all_gather | solution.py:54
  379.5 9.1 %fusion.11 = f32[1024,1024]{1,0:T(8,128)} fusion(bf16[1024,1792]{1,0:T(8,128)(2,1)} %all-gather.13.cloned.1.call-done, bf16[1024,1792]{1,0:T(8,128)(2,1)} %all-gather.15.cloned.1.call-done), kind=kOutput, calls=%fused_computation.25 | convolution fusion | flops 3758096384 | bytes 11534336 | tf_op jit(solution)/shard_map/dot_general | solution.py:23
  388.7 27.5 %all-gather.19.cloned.1.call-done = bf16[1024,1792]{1,0:T(8,128)(2,1)} async-done(((bf16[256,1792]{1,0:T(8,128)(2,1)}), bf16[1024,1792]{1,0:T(8,128)(2,1)}) %all-gather.19.cloned.1.call-update) | async-done | bytes 3670032 | tf_op jit(solution)/shard_map/all_gather | solution.py:56
  416.1 9.7 %add_convert_fusion = bf16[1024,1024]{1,0:T(8,128)(2,1)} fusion(f32[1024,1024]{1,0:T(8,128)} %fusion.11, bf16[1024,1792]{1,0:T(8,128)(2,1)} %all-gather.17.cloned.1.call-done, bf16[1024,1792]{1,0:T(8,128)(2,1)} %all-gather.19.cloned.1.call-done), kind=kOutput, calls=%fused_computation | convolution fusion | flops 3760193536 | bytes 13631488 | tf_op jit(solution)/shard_map/dot_general | solution.py:23
  425.9 40.3 %reduce-scatter.10.cloned.1.call-done = bf16[256,1792]{0,1:T(8,128)(2,1)} async-done(((bf16[1024,1792]{0,1:T(8,128)(2,1)}), bf16[256,1792]{0,1:T(8,128)(2,1)}) %reduce-scatter.10.cloned.1.call-update) | async-done | bytes 917520 | tf_op jit(solution)/shard_map/reduce_scatter | solution.py:59
  466.2 1.4 multiply_convert_fusion.2
  467.5 1.4 copy.11
  468.9 47.6 %reduce-scatter.12.cloned.1.call-done = bf16[256,1792]{0,1:T(8,128)(2,1)} async-done(((bf16[1024,1792]{0,1:T(8,128)(2,1)}), bf16[256,1792]{0,1:T(8,128)(2,1)}) %reduce-scatter.12.cloned.1.call-update) | async-done | bytes 917520 | tf_op jit(solution)/shard_map/reduce_scatter | solution.py:66
  517.9 1.4 copy.12
  519.3 47.3 %reduce-scatter.14.cloned.1.call-done = bf16[1792,256]{1,0:T(8,128)(2,1)} async-done(((bf16[1792,1024]{1,0:T(8,128)(2,1)}), bf16[1792,256]{1,0:T(8,128)(2,1)}) %reduce-scatter.14.cloned.1.call-update) | async-done | bytes 917520 | tf_op jit(solution)/shard_map/reduce_scatter | solution.py:76
  566.6 2.3 multiply_convert_fusion
  568.9 52.2 %reduce-scatter.8.cloned.1.call-done = bf16[128,1024]{1,0:T(8,128)(2,1)} async-done(((bf16[1024,1024]{1,0:T(8,128)(2,1)}), bf16[128,1024]{1,0:T(8,128)(2,1)}) %reduce-scatter.8.cloned.1.call-update) | async-done | bytes 262160 | tf_op jit(solution)/shard_map/reduce_scatter | solution.py:72
  (35 shorter events, 6.7 us)
Async XLA Ops:
  7.2 55.6 %all-gather.9.cloned.1.call-start = ((), (), s32[]{:S(2)}) async-start(), calls=%async_computation.5 | async-start | bytes 2359296 | tf_op jit(solution)/shard_map/all_gather | solution.py:37
  7.9 92.2 %all-gather.11.cloned.1.call-start = ((), (), s32[]{:S(2)}) async-start(), calls=%async_computation.6 | async-start | bytes 4587520 | tf_op jit(solution)/shard_map/all_gather | solution.py:39
  8.6 142.7 %reduce-scatter.6.cloned.1.call-start = ((), (), s32[]{:S(2)}) async-start(), calls=%async_computation.7 | async-start | bytes 4587520 | tf_op jit(solution)/shard_map/reduce_scatter | solution.py:40
  108.5 42.8 %copy-start = (bf16[256,1792]{1,0:T(8,128)(2,1)S(1)}, bf16[256,1792]{1,0:T(8,128)(2,1)}, u32[]{:S(2)}) copy-start(bf16[256,1792]{1,0:T(8,128)(2,1)} %param.10) | copy-start | bytes 2752516
  108.5 42.8 %copy-start.1 = (bf16[256,1792]{1,0:T(8,128)(2,1)S(1)}, bf16[256,1792]{1,0:T(8,128)(2,1)}, u32[]{:S(2)}) copy-start(bf16[256,1792]{1,0:T(8,128)(2,1)} %param.9) | copy-start | bytes 2752516
  108.6 95.1 %all-gather.21.cloned.1.call-start = ((), (), s32[]{:S(2)}) async-start(), calls=%async_computation.13 | async-start | bytes 2359296 | tf_op jit(solution)/shard_map/all_gather | solution.py:36
  109.1 140.9 %all-gather.13.cloned.1.call-start = ((), (), s32[]{:S(2)}) async-start(), calls=%async_computation.8 | async-start | bytes 4587520 | tf_op jit(solution)/shard_map/all_gather | solution.py:48
  155.1 141.2 %all-gather.17.cloned.1.call-start = ((), (), s32[]{:S(2)}) async-start(), calls=%async_computation.10 | async-start | bytes 4587520 | tf_op jit(solution)/shard_map/all_gather | solution.py:49
  155.7 187.1 %all-gather.23.cloned.1.call-start = ((), (), s32[]{:S(2)}) async-start(), calls=%async_computation.16 | async-start | bytes 4587520 | tf_op jit(solution)/shard_map/all_gather | solution.py:50
  156.4 223.1 %all-gather.15.cloned.1.call-start = ((), (), s32[]{:S(2)}) async-start(), calls=%async_computation.9 | async-start | bytes 4587520 | tf_op jit(solution)/shard_map/all_gather | solution.py:54
  157.2 258.9 %all-gather.19.cloned.1.call-start = ((), (), s32[]{:S(2)}) async-start(), calls=%async_computation.11 | async-start | bytes 4587520 | tf_op jit(solution)/shard_map/all_gather | solution.py:56
  157.9 308.2 %reduce-scatter.10.cloned.1.call-start = ((), (), s32[]{:S(2)}) async-start(), calls=%async_computation.14 | async-start | bytes 4587520 | tf_op jit(solution)/shard_map/reduce_scatter | solution.py:59
  258.6 37.7 %copy-start.3 = (bf16[1024,1024]{1,0:T(8,128)(2,1)S(1)}, bf16[1024,1024]{1,0:T(8,128)(2,1)}, u32[]{:S(2)}) copy-start(bf16[1024,1024]{1,0:T(8,128)(2,1)} %all-gather.21.cloned.1.call-done) | copy-start | bytes 6291460
  258.7 257.9 %reduce-scatter.12.cloned.1.call-start = ((), (), s32[]{:S(2)}) async-start(), calls=%async_computation.15 | async-start | bytes 4587520 | tf_op jit(solution)/shard_map/reduce_scatter | solution.py:66
  303.9 38.9 %copy-start.2 = (bf16[1024,1024]{1,0:T(8,128)(2,1)S(1)}, bf16[1024,1024]{1,0:T(8,128)(2,1)}, u32[]{:S(2)}) copy-start(bf16[1024,1024]{1,0:T(8,128)(2,1)} %all-gather.9.cloned.1.call-done) | copy-start | bytes 6291460
  304.0 262.6 %reduce-scatter.14.cloned.1.call-start = ((), (), s32[]{:S(2)}) async-start(), calls=%async_computation.17 | async-start | bytes 4587520 | tf_op jit(solution)/shard_map/reduce_scatter | solution.py:76
  350.4 270.7 %reduce-scatter.8.cloned.1.call-start = ((), (), s32[]{:S(2)}) async-start(), calls=%async_computation.12 | async-start | bytes 2359296 | tf_op jit(solution)/shard_map/reduce_scatter | solution.py:72
Sparse Core Ops, SparseCore 0:
  9.6 53.0 all-gather.8
  64.4 35.6 all-gather.10
  108.7 42.6 reduce-scatter.5
  152.8 50.7 all-gather.20
  205.7 44.3 all-gather.12
  252.1 44.1 all-gather.16
  298.6 44.1 all-gather.22
  344.5 35.0 all-gather.14
  381.2 34.8 all-gather.18
  418.6 47.4 reduce-scatter.9
  469.0 47.4 reduce-scatter.11
  519.0 47.4 reduce-scatter.13
  569.7 51.3 reduce-scatter.7
where the time goes:
time: 629 us; the launch traced here: 628 us
  waiting for transfers between devices  550 us (87%)
  matrix products  51 us (8%)
  between operations  13.9 us (2%)
  other arithmetic  8.71 us (1%)
    all_gather x1, waiting for transfers between devices, shards(): lax.all_gather(grad_out, 'row', axis=0, tiled=True)  54 us
    reduce_scatter x1, waiting for transfers between devices, shards(): lax.psum_scatter(partial_in.astype(jnp.bfloat16), 'row', scatter_dimensio...  52.2 us
    reduce_scatter x1, waiting for transfers between devices, shards(): lax.psum_scatter(contract_first(token_cols, up_whole).astype(jnp.bfloat16...  47.6 us
    reduce_scatter x1, waiting for transfers between devices, shards(): lax.psum_scatter(down_term.astype(jnp.bfloat16), 'depth', scatter_dimensi...  47.3 us
    all_gather x1, waiting for transfers between devices, shards(): lax.all_gather(grad_gate, 'col', axis=0, tiled=True)  46.4 us
    all_gather x1, waiting for transfers between devices, shards(): lax.all_gather(tokens_in, 'row', axis=0, tiled=True)  45.6 us
    reduce_scatter x1, waiting for transfers between devices, shards(): lax.psum_scatter(contract_last(grad_whole, down_whole).astype(jnp.bfloat1...  42.2 us
    reduce_scatter x1, waiting for transfers between devices, shards(): lax.psum_scatter(contract_first(token_cols, gate_whole).astype(jnp.bfloat...  40.3 us
  transfers between devices with their start and end apart: 13, of which 13 were waited for; matrix products, arithmetic and copies ran while one was open for 9% of the time, Pallas kernels for 0%

commit v1 on v0

v1 whole, which is shorter than its diff:
```python
import functools
import math

import jax
import jax.numpy as jnp
from jax import lax
from jax.experimental import pallas as pl
from jax.experimental.pallas import tpu as pltpu
from jax.sharding import PartitionSpec as P

MESH = pl.DeviceIdType.MESH
BF = jnp.bfloat16
F32 = jnp.float32
NC = 7
CH = 256
AHEAD = 3


def dot_nt(a, b):
    return lax.dot_general(a, b, (((1,), (1,)), ((), ())), preferred_element_type=F32)


def dot_nn(a, b):
    return lax.dot_general(a, b, (((1,), (0,)), ((), ())), preferred_element_type=F32)


def remote(src, dst, ssem, rsem, dev):
    return pltpu.make_async_remote_copy(
        src_ref=src, dst_ref=dst, send_sem=ssem, recv_sem=rsem, device_id=dev, device_id_type=MESH
    )


def kernel(
    scale,
    tok_in, go_in, gp_in, up_in, gw_in, uw_in, dw_in,
    gin_out, ggw_out, guw_out, gdw_out, tkl,
    go, tkt, dw, wgu, gpu, rs1s, rs1r, rs2s, rs2r, nb, own, hid, ggu, ac, act, acc, pin, gr,
    cs, cr, opart, zs, zr, oq,
    loc, go_s, go_r, tk_s, tk_r, dw_s, dw_r, wg_s, wg_r, gp_s, gp_r,
    rs1_s, rs1_m, rs2_s, rs2_m, ag1_s, ag1_m, ag2_s, ag2_m, c_s, c_m, z_s, z_m, gi_s, gi_m,
):
    dep = lax.axis_index("depth")
    row = lax.axis_index("row")
    y = lax.axis_index("col")
    zh, co = dep // 2, dep % 2
    x, zl = row // 2, row % 2
    yp, ym, yo = (y + 1) % 4, (y + 3) % 4, (y + 2) % 4
    up_dev = (dep, row, yp)
    dn_dev = (dep, row, ym)
    zhi_dep = (1 - zh) * 2 + co
    core_dep = zh * 2 + (1 - co)
    zhi_dev = (zhi_dep, row, y)
    core_dev = (core_dep, row, y)
    zlo_row = x * 2 + (1 - zl)
    zlo_dev = (dep, zlo_row, y)
    xs = [((x + d) % 4) * 2 + zl for d in (1, 3, 2)]
    x_dev = [(dep, r, y) for r in xs]

    def wait_recv(ref, sem, dev):
        remote(ref, ref, sem, sem, dev).wait_recv()

    def wait_send(ref, sem, dev):
        remote(ref, ref, sem, sem, dev).wait_send()

    def rows(r, n):
        return pl.ds(pl.multiple_of(r * n, n), n)

    l_go = pltpu.make_async_copy(go_in, go.at[rows(row, 128)], loc.at[0])
    l_dw = pltpu.make_async_copy(dw_in, dw.at[:, rows(dep, 256)], loc.at[1])
    l_tk = pltpu.make_async_copy(tok_in, tkl.at[rows(row, 128)], loc.at[2])
    l_go.start()
    l_dw.start()

    def l_gp(j):
        c = pl.ds(j * CH, CH)
        return (
            pltpu.make_async_copy(gp_in.at[:, c], gpu.at[j, y, 0], loc.at[4 + j]),
            pltpu.make_async_copy(up_in.at[:, c], gpu.at[j, y, 1], loc.at[11 + j]),
        )

    def l_wg(j):
        c = pl.ds(j * CH, CH)
        return (
            pltpu.make_async_copy(gw_in.at[:, c], wgu.at[j, rows(dep, 256), 0:CH], loc.at[18 + j]),
            pltpu.make_async_copy(
                uw_in.at[:, c], wgu.at[j, rows(dep, 256), CH : 2 * CH], loc.at[25 + j]
            ),
        )

    for j in range(NC):
        for c in l_gp(j):
            c.start()
    for j in range(NC):
        for c in l_wg(j):
            c.start()
    l_tk.start()

    barrier = pltpu.get_barrier_semaphore()
    peers = [up_dev, dn_dev, zhi_dev, core_dev]
    for d in range(1, 8):
        peers.append((dep, (row + d) % 8, y))
    for dev in peers:
        pl.semaphore_signal(barrier, inc=1, device_id=dev, device_id_type=MESH)
    pl.semaphore_wait(barrier, len(peers))

    def row_sends(buf, ssem, rsem, r, which):
        ref = buf.at[rows(r, 128)]
        cps = [remote(ref, ref, ssem.at[which, i], rsem.at[r], x_dev[i]) for i in range(3)]
        if which == 0:
            cps.append(remote(ref, ref, ssem.at[0, 3], rsem.at[r], zlo_dev))
        return cps

    def dw_ref(p):
        return dw.at[:, rows(p, 256)]

    def wg_ref(j, p):
        return wgu.at[j, rows(p, 256)]

    def gp_step1(j):
        ref = gpu.at[j, y]
        return (
            remote(ref, ref, gp_s.at[j, 0], gp_r.at[j, 0], up_dev),
            remote(ref, ref, gp_s.at[j, 1], gp_r.at[j, 1], dn_dev),
        )

    def gp_step2(j):
        a, b = gpu.at[j, ym, 0], gpu.at[j, yp, 1]
        return (
            remote(a, a, gp_s.at[j, 2], gp_r.at[j, 2], up_dev),
            remote(b, b, gp_s.at[j, 3], gp_r.at[j, 3], dn_dev),
        )

    def gp_relay(j):
        f, s = gp_step2(j)
        wait_recv(gpu.at[j, ym], gp_r.at[j, 0], dn_dev)
        f.start()
        wait_recv(gpu.at[j, yp], gp_r.at[j, 1], up_dev)
        s.start()

    def wg_send(j):
        ref = wg_ref(j, dep)
        return (
            remote(ref, ref, wg_s.at[j, 0], wg_r.at[j, 0], zhi_dev),
            remote(ref, ref, wg_s.at[j, 1], wg_r.at[j, 1], core_dev),
        )

    def wg_fwd(j):
        ref = wg_ref(j, zhi_dep)
        return remote(ref, ref, wg_s.at[j, 2], wg_r.at[j, 2], core_dev)

    l_go.wait()
    for c in row_sends(go, go_s, go_r, row, 0):
        c.start()
    l_dw.wait()
    ref = dw_ref(dep)
    dw_a = remote(ref, ref, dw_s.at[0], dw_r.at[0], zhi_dev)
    dw_b = remote(ref, ref, dw_s.at[1], dw_r.at[1], core_dev)
    dw_a.start()
    dw_b.start()
    for j in range(NC):
        for c in l_gp(j):
            c.wait()
        if j < AHEAD:
            for c in gp_step1(j):
                c.start()
    wait_recv(go.at[rows(zlo_row, 128)], go_r.at[zlo_row], zlo_dev)
    for c in row_sends(go, go_s, go_r, zlo_row, 1):
        c.start()
    for j in range(NC):
        for c in l_wg(j):
            c.wait()
    l_tk.wait()
    acc[...] = jnp.zeros_like(acc)
    for j in range(AHEAD):
        gp_relay(j)
        if j == 1:
            for c in row_sends(tkl, tk_s, tk_r, row, 0):
                c.start()
    wait_recv(dw_ref(zhi_dep), dw_r.at[0], zhi_dev)
    ref = dw_ref(zhi_dep)
    dw_c = remote(ref, ref, dw_s.at[2], dw_r.at[2], core_dev)
    dw_c.start()
    for j in range(2):
        for c in wg_send(j):
            c.start()
    wait_recv(dw_ref(core_dep), dw_r.at[1], core_dev)
    for i in range(3):
        wait_recv(go.at[rows(xs[i], 128)], go_r.at[xs[i]], x_dev[i])
    for d in (1, 3, 2):
        r = ((x + d) % 4) * 2 + (1 - zl)
        wait_recv(go.at[rows(r, 128)], go_r.at[r], zlo_dev)
    wait_recv(dw_ref((1 - zh) * 2 + (1 - co)), dw_r.at[2], core_dev)

    def rs1_copies(k):
        return (
            remote(rs1s.at[k, 0:128], rs1r.at[k, 0], rs1_s.at[k, 0], rs1_m.at[k, 0], up_dev),
            remote(rs1s.at[k, 128:256], rs1r.at[k, 1], rs1_s.at[k, 1], rs1_m.at[k, 1], dn_dev),
        )

    def rs2_copies(k):
        return (
            remote(rs2s.at[k, 0], rs2r.at[k, 0], rs2_s.at[k, 0], rs2_m.at[k, 0], up_dev),
            remote(rs2s.at[k, 1], rs2r.at[k, 1], rs2_s.at[k, 1], rs2_m.at[k, 1], dn_dev),
        )

    def ag1_copies(k):
        ref = hid.at[k, y]
        return (
            remote(ref, ref, ag1_s.at[k, 0], ag1_m.at[k, 0], up_dev),
            remote(ref, ref, ag1_s.at[k, 1], ag1_m.at[k, 1], dn_dev),
        )

    def ag2_copies(k):
        a, b = hid.at[k, ym, 0:128], hid.at[k, yp, 128:256]
        return (
            remote(a, a, ag2_s.at[k, 0], ag2_m.at[k, 0], up_dev),
            remote(b, b, ag2_s.at[k, 1], ag2_m.at[k, 1], dn_dev),
        )

    def stage_a(k):
        w = dw[rows(k, CH), :]

        def part(q):
            return dot_nt(go[rows(q, 256), :], w)

        rs1s[k] = part(yo).astype(BF)
        for c in rs1_copies(k):
            c.start()
        nb[0] = part(yp)
        nb[1] = part(ym)
        own[k % 2] = part(y)

    def stage_b(k):
        wait_recv(rs1r.at[k, 0], rs1_m.at[k, 0], dn_dev)
        f, s = rs2_copies(k)
        rs2s[k, 0, 0:128] = (nb[0, 0:128] + rs1r[k, 0].astype(F32)).astype(BF)
        rs2s[k, 0, 128:256] = nb[0, 128:256].astype(BF)
        f.start()
        wait_recv(rs1r.at[k, 1], rs1_m.at[k, 1], up_dev)
        rs2s[k, 1, 0:128] = nb[1, 0:128].astype(BF)
        rs2s[k, 1, 128:256] = (nb[1, 128:256] + rs1r[k, 1].astype(F32)).astype(BF)
        s.start()

    def stage_c(k):
        wait_recv(rs2r.at[k, 0], rs2_m.at[k, 0], dn_dev)
        wait_recv(rs2r.at[k, 1], rs2_m.at[k, 1], up_dev)
        hid[k, y] = (own[k % 2] + rs2r[k, 0].astype(F32) + rs2r[k, 1].astype(F32)).astype(BF)
        for c in ag1_copies(k):
            c.start()

    def stage_d(k):
        f, s = ag2_copies(k)
        wait_recv(hid.at[k, ym], ag1_m.at[k, 0], dn_dev)
        f.start()
        wait_recv(hid.at[k, yp], ag1_m.at[k, 1], up_dev)
        s.start()

    def core_copy(j):
        return remote(cs.at[j % 2], cr.at[j], c_s.at[j], c_m.at[j], core_dev)

    def z_copy(j):
        return remote(zs.at[j % 2], zr.at[j], z_s.at[j], z_m.at[j], zhi_dev)

    def grad_parts(p):
        a = dot_nn(tkt[rows(p, 256), :], ggu[...])
        b = dot_nn(act[...], go[:, rows(p, 256)])
        return a, b

    def stage_e1(j):
        wait_recv(gpu.at[j, yo, 0], gp_r.at[j, 2], dn_dev)
        wait_recv(gpu.at[j, yo, 1], gp_r.at[j, 3], up_dev)
        wait_recv(hid.at[j, yo, 0:128], ag2_m.at[j, 0], dn_dev)
        wait_recv(hid.at[j, yo, 128:256], ag2_m.at[j, 1], up_dev)

        @pl.loop(0, 16)
        def _(i):
            c = i // 4
            r = pl.ds(pl.multiple_of((i % 4) * 64, 64), 64)
            o = pl.ds(pl.multiple_of(i * 64, 64), 64)
            h = hid[j, c, r, :].astype(F32)
            g = gpu[j, c, 0, r, :].astype(F32)
            u = gpu[j, c, 1, r, :].astype(F32)
            s = jax.nn.sigmoid(g)
            w = g * s
            ac[o, :] = (w * u).astype(BF)
            ggu[o, 0:CH] = (h * u * s * (1.0 + g * (1.0 - s))).astype(BF)
            ggu[o, CH : 2 * CH] = (h * w).astype(BF)

        for c in range(4):
            act[:, c * 256 : (c + 1) * 256] = ac[c * 256 : (c + 1) * 256, :].T

        @pl.when(j >= 2)
        def _():
            core_copy(j - 2).wait_send()

        @pl.loop(0, 2)
        def _(h):
            a, b = grad_parts(h * 2 + (1 - co))
            cs[j % 2, h, :, 0 : 2 * CH] = a.astype(BF)
            cs[j % 2, h, :, 2 * CH : 3 * CH] = b.astype(BF)

        core_copy(j).start()

        @pl.loop(0, 2)
        def _(h):
            a, b = grad_parts(h * 2 + co)
            opart[h, :, 0 : 2 * CH] = a
            opart[h, :, 2 * CH : 3 * CH] = b

    def gi_copy(d):
        r = (row + d) % 8
        return remote(
            pin.at[rows(r, 128)], gr.at[row], gi_s.at[d], gi_m.at[row], (dep, r, y)
        )

    def stage_e2(j):
        wait_recv(wg_ref(j, zhi_dep), wg_r.at[j, 0], zhi_dev)
        wg_fwd(j).start()
        wait_recv(wg_ref(j, core_dep), wg_r.at[j, 1], core_dev)
        wait_recv(wg_ref(j, (1 - zh) * 2 + (1 - co)), wg_r.at[j, 2], core_dev)

        @pl.loop(0, 4)
        def _(q):
            o = rows(q, 256)
            acc[o, :] += dot_nt(ggu[o, :], wgu[j])

    def stage_f(j):
        @pl.when(j >= 2)
        def _():
            z_copy(j - 2).wait_send()

        wait_recv(cr.at[j], c_m.at[j], core_dev)
        zs[j % 2] = (opart[1 - zh] + cr[j, 1 - zh].astype(F32)).astype(BF)
        z_copy(j).start()
        oq[j % 2] = opart[zh] + cr[j, zh].astype(F32)

    def stage_g(j):
        wait_recv(zr.at[j], z_m.at[j], zhi_dev)
        t = (oq[j % 2] + zr[j].astype(F32)) * scale
        c = rows(j, CH)
        ggw_out[:, c] = t[:, 0:CH].astype(BF)
        guw_out[:, c] = t[:, CH : 2 * CH].astype(BF)
        gdw_out[c, :] = t[:, 2 * CH : 3 * CH].astype(BF)

    def when(cond):
        return pl.when(cond)

    def body(k, carry):
        @when(k < NC)
        def _():
            stage_a(k)

        @when((k >= 1) & (k < NC + 1))
        def _():
            stage_c(k - 1)

        @when((k >= AHEAD - 2) & (k + 2 < NC))
        def _():
            for c in gp_step1(k + 2):
                c.start()

        @when(k + 2 < NC)
        def _():
            for c in wg_send(k + 2):
                c.start()

        @when(k == 0)
        def _():
            wait_recv(tkl.at[rows(zlo_row, 128)], tk_r.at[zlo_row], zlo_dev)
            for c in row_sends(tkl, tk_s, tk_r, zlo_row, 1):
                c.start()

        @when((k >= 3) & (k < NC + 3))
        def _():
            stage_f(k - 3)

        @when((k >= 2) & (k < NC + 2))
        def _():
            stage_e1(k - 2)

        @when(k < NC)
        def _():
            stage_b(k)

        @when((k >= 1) & (k < NC + 1))
        def _():
            stage_d(k - 1)

        @when((k >= AHEAD - 2) & (k + 2 < NC))
        def _():
            gp_relay(k + 2)

        @when(k == 1)
        def _():
            for i in range(3):
                wait_recv(tkl.at[rows(xs[i], 128)], tk_r.at[xs[i]], x_dev[i])
            for d in (1, 3, 2):
                r = ((x + d) % 4) * 2 + (1 - zl)
                wait_recv(tkl.at[rows(r, 128)], tk_r.at[r], zlo_dev)
            cp = pltpu.make_async_copy(tkl, pin, loc.at[3])
            cp.start()
            cp.wait()

            @pl.loop(0, 4)
            def _(q):
                o = rows(q, 256)
                tkt[:, o] = pin[o, :].T

        @when((k >= 2) & (k < NC + 2))
        def _():
            stage_e2(k - 2)

        @when(k == NC + 1)
        def _():
            pin[...] = acc[...].astype(BF)
            for d in (4, 3, 5, 2, 6, 1, 7):
                gi_copy(d).start()

        @when(k >= 4)
        def _():
            stage_g(k - 4)

        return carry

    lax.fori_loop(0, NC + 4, body, 0)

    total = acc[rows(row, 128), :]
    for d in (1, 7, 2, 6, 3, 5, 4):
        r = (row + d) % 8
        wait_recv(gr.at[r], gi_m.at[r], (dep, r, y))
        total = total + gr[r].astype(F32)
    gin_out[...] = total.astype(BF)

    for c in row_sends(go, go_s, go_r, row, 0) + row_sends(go, go_s, go_r, zlo_row, 1):
        c.wait_send()
    for c in row_sends(tkl, tk_s, tk_r, row, 0) + row_sends(tkl, tk_s, tk_r, zlo_row, 1):
        c.wait_send()
    dw_a.wait_send()
    dw_b.wait_send()
    dw_c.wait_send()
    for d in range(1, 8):
        gi_copy(d).wait_send()

    def drain(j, carry):
        for c in (*gp_step1(j), *gp_step2(j), *wg_send(j), wg_fwd(j), *rs1_copies(j)):
            c.wait_send()
        for c in (*rs2_copies(j), *ag1_copies(j), *ag2_copies(j)):
            c.wait_send()

        @pl.when(j >= NC - 2)
        def _():
            core_copy(j).wait_send()
            z_copy(j).wait_send()

        return carry

    lax.fori_loop(0, NC, drain, 0)


def shards(tokens_in, grad_out, gate_pre, up_pre, gate_weight, up_weight, down_weight):
    scale = 1.0 / math.sqrt(4096.0)
    dma = pltpu.SemaphoreType.DMA
    vm = pltpu.VMEM
    hbm = pl.BlockSpec(memory_space=pl.ANY)
    vmem = pl.BlockSpec(memory_space=pltpu.VMEM)
    outs = pl.pallas_call(
        functools.partial(kernel, scale),
        out_shape=[
            jax.ShapeDtypeStruct((128, 1024), BF),
            jax.ShapeDtypeStruct((256, 1792), BF),
            jax.ShapeDtypeStruct((256, 1792), BF),
            jax.ShapeDtypeStruct((1792, 256), BF),
            jax.ShapeDtypeStruct((1024, 1024), BF),
        ],
        in_specs=[hbm] * 7,
        out_specs=[vmem] * 4 + [hbm],
        scratch_shapes=[
            vm((1024, 1024), BF),
            vm((1024, 1024), BF),
            vm((1792, 1024), BF),
            vm((NC, 1024, 2 * CH), BF),
            vm((NC, 4, 2, 256, CH), BF),
            vm((NC, 256, CH), BF),
            vm((NC, 2, 128, CH), BF),
            vm((NC, 2, 256, CH), BF),
            vm((NC, 2, 256, CH), BF),
            vm((2, 256, CH), F32),
            vm((2, 256, CH), F32),
            vm((NC, 4, 256, CH), BF),
            vm((1024, 2 * CH), BF),
            vm((1024, CH), BF),
            vm((CH, 1024), BF),
            vm((1024, 1024), F32),
            vm((1024, 1024), BF),
            vm((8, 128, 1024), BF),
            vm((2, 2, 256, 3 * CH), BF),
            vm((NC, 2, 256, 3 * CH), BF),
            vm((2, 256, 3 * CH), F32),
            vm((2, 256, 3 * CH), BF),
            vm((NC, 256, 3 * CH), BF),
            vm((2, 256, 3 * CH), F32),
            dma((32,)),
            dma((2, 4)), dma((8,)),
            dma((2, 4)), dma((8,)),
            dma((3,)), dma((3,)),
            dma((NC, 3)), dma((NC, 3)),
            dma((NC, 4)), dma((NC, 4)),
            dma((NC, 2)), dma((NC, 2)),
            dma((NC, 2)), dma((NC, 2)),
            dma((NC, 2)), dma((NC, 2)),
            dma((NC, 2)), dma((NC, 2)),
            dma((NC,)), dma((NC,)),
            dma((NC,)), dma((NC,)),
            dma((8,)), dma((8,)),
        ],
        compiler_params=pltpu.CompilerParams(
            collective_id=0, has_side_effects=True, vmem_limit_bytes=62 * 2**20
        ),
        cost_estimate=pl.CostEstimate(
            flops=22_500_000_000, bytes_accessed=20_000_000, transcendentals=2_000_000
        ),
        name="swiglu_backward",
    )(tokens_in, grad_out, gate_pre, up_pre, gate_weight, up_weight, down_weight)
    return tuple(outs[:4])


def solution(mesh):
    return jax.shard_map(
        shards,
        mesh=mesh,
        in_specs=(
            P(("depth", "row"), "col"),
            P(("depth", "row"), "col"),
            P(("depth", "col"), "row"),
            P(("depth", "col"), "row"),
            P(("col", "depth"), "row"),
            P(("col", "depth"), "row"),
            P("row", ("col", "depth")),
        ),
        out_specs=(
            P(("depth", "row"), "col"),
            P(("col", "depth"), "row"),
            P(("col", "depth"), "row"),
            P("row", ("col", "depth")),
        ),
        check_vma=False,
    )
```

time: 629 us -> 197 us (0.31)
  waiting for transfers between devices: 550 us -> 0 us
  Pallas kernels: 0 us -> 187 us
  matrix products: 51 us -> 0 us
  between operations: 13.9 us -> 0.66 us
  other arithmetic: 8.71 us -> 0 us
    all_gather x8 -> x0, waiting for transfers between devices: 316 us -> none  [the longest x1 54 us: shards(): lax.all_gather(grad_out, 'row', axis=0, tiled=True)]
    reduce_scatter x5 -> x0, waiting for transfers between devices: 230 us -> none  [the longest x1 52.2 us: shards(): lax.psum_scatter(partial_in.astype(jnp.bfloat16), 'row', scatter_dimensio...]
    pallas_call x0 -> x1, Pallas kernels: none -> 187 us  [shards(): pl.pallas_call(functools.partial(kernel, scale), out_shape=[jax.ShapeDtyp...]
    dot_general x6 -> x0, matrix products: 51 us -> none  [the longest x3 27.3 us: contract_last(): lax.dot_general(left, right, (((1,), (1,)), ((), ())), preferred_element_...]
    convert_element_type x4 -> x0, other arithmetic: 8.71 us -> none  [the longest x1 3.74 us: backward_gates(): activ = (swish_value * up_value).astype(jnp.bfloat16)]
  transfers between devices with their start and end apart: 13 -> 0, of which waited for: 13 -> 0; matrix products, arithmetic and copies ran while one was open for 9% -> 0% of each run, Pallas kernels for 0% -> 0%
where the time goes in v1:
time: 197 us; the launch traced here: 194 us
  Pallas kernels  187 us (95%)
  local copies, waits for them, and re-layouts  5.81 us (3%)
    pallas_call x1, Pallas kernels, shards(): pl.pallas_call(functools.partial(kernel, scale), out_shape=[jax.ShapeDtyp...  187 us
    unnamed x8, local copies, waits for them, and re-layouts  5.81 us

profile of v1, /device:TPU:32, one launch (start us, length us, event | category | flops | bytes accessed | tf_op | source)
XLA Modules:
  0.0 193.9 jit_solution(12453060754182670172)
XLA Ops:
  0.6 187.4 %swiglu_backward.1 = (bf16[128,1024]{1,0:T(8,128)(2,1)}, bf16[256,1792]{1,0:T(8,128)(2,1)}, bf16[256,1792]{1,0:T(8,128)(2,1)}, bf16[1792,256]{1,0:T(8,128)(2,1)}, bf16[1024,1024]{1,0:T(8,128)(2,1)}) custom-call(bf16[128,1024]{1,0:T(8,128)(2,1)} %tok_in.1, bf16[128,1024]{1,0:T(8,128)(2,1)} %go_in.1, bf16[256,1792]{1,0:T(8,128)(2,1)} %gp_in.1, ...), custom_call_target="tpu_custom_call" | custom-call | flops 22499999744 | bytes 20000000 | tf_op jit(solution)/shard_map/swiglu_backward/pallas_call | solution.py:466
  188.1 0.0 copy-start.1
  188.1 0.0 copy-start
  188.1 1.8 copy.15
  189.9 2.2 %copy.16 = bf16[256,1792]{1,0:T(8,128)(2,1)} copy(bf16[256,1792]{1,0:T(8,128)(2,1)} %get-tuple-element.17) | data formatting | bytes 1835008
  192.1 0.0 copy-done.1
  192.1 0.9 copy.17
  193.0 0.0 copy-done
  193.0 0.9 copy.18
Async XLA Ops:
  188.1 4.0 %copy-start.1 = (bf16[256,1792]{1,0:T(8,128)(2,1)S(1)}, bf16[256,1792]{1,0:T(8,128)(2,1)}, u32[]{:S(2)}) copy-start(bf16[256,1792]{1,0:T(8,128)(2,1)} %get-tuple-element.18) | copy-start | bytes 2752516
  188.1 4.9 %copy-start = (bf16[1792,256]{1,0:T(8,128)(2,1)S(1)}, bf16[1792,256]{1,0:T(8,128)(2,1)}, u32[]{:S(2)}) copy-start(bf16[1792,256]{1,0:T(8,128)(2,1)} %get-tuple-element.19) | copy-start | bytes 2752516

commit v2 on v1

--- a/solution.py
+++ b/solution.py
@@ -13,7 +13,7 @@
 F32 = jnp.float32
 NC = 7
 CH = 256
-AHEAD = 3
+AHEAD = 4
 
 
 def dot_nt(a, b):
@@ -33,11 +33,11 @@
 def kernel(
     scale,
     tok_in, go_in, gp_in, up_in, gw_in, uw_in, dw_in,
-    gin_out, ggw_out, guw_out, gdw_out, tkl,
-    go, tkt, dw, wgu, gpu, rs1s, rs1r, rs2s, rs2r, nb, own, hid, ggu, ac, act, acc, pin, gr,
+    gin_out, ggw_out, guw_out, gdw_out,
+    go, tkt, dw, wgu, gpu, rs1s, rs1r, rs2s, rs2r, nb, own, hid, ggu, ac, act, acc, pin, g1, g2, gs, gz,
     cs, cr, opart, zs, zr, oq,
     loc, go_s, go_r, tk_s, tk_r, dw_s, dw_r, wg_s, wg_r, gp_s, gp_r,
-    rs1_s, rs1_m, rs2_s, rs2_m, ag1_s, ag1_m, ag2_s, ag2_m, c_s, c_m, z_s, z_m, gi_s, gi_m,
+    rs1_s, rs1_m, rs2_s, rs2_m, ag1_s, ag1_m, ag2_s, ag2_m, c_s, c_m, z_s, z_m, gi_s, gi_m, gz_s, gz_m,
 ):
     dep = lax.axis_index("depth")
     row = lax.axis_index("row")
@@ -67,9 +67,7 @@
 
     l_go = pltpu.make_async_copy(go_in, go.at[rows(row, 128)], loc.at[0])
     l_dw = pltpu.make_async_copy(dw_in, dw.at[:, rows(dep, 256)], loc.at[1])
-    l_tk = pltpu.make_async_copy(tok_in, tkl.at[rows(row, 128)], loc.at[2])
-    l_go.start()
-    l_dw.start()
+    l_tk = pltpu.make_async_copy(tok_in, pin.at[rows(row, 128)], loc.at[2])
 
     def l_gp(j):
         c = pl.ds(j * CH, CH)
@@ -87,7 +85,11 @@
             ),
         )
 
-    for j in range(NC):
+    l_go.start()
+    for c in l_gp(0):
+        c.start()
+    l_dw.start()
+    for j in range(1, NC):
         for c in l_gp(j):
             c.start()
     for j in range(NC):
@@ -151,13 +153,17 @@
     l_go.wait()
     for c in row_sends(go, go_s, go_r, row, 0):
         c.start()
+    for c in l_gp(0):
+        c.wait()
+    for c in gp_step1(0):
+        c.start()
     l_dw.wait()
     ref = dw_ref(dep)
     dw_a = remote(ref, ref, dw_s.at[0], dw_r.at[0], zhi_dev)
     dw_b = remote(ref, ref, dw_s.at[1], dw_r.at[1], core_dev)
     dw_a.start()
     dw_b.start()
-    for j in range(NC):
+    for j in range(1, NC):
         for c in l_gp(j):
             c.wait()
         if j < AHEAD:
@@ -174,13 +180,13 @@
     for j in range(AHEAD):
         gp_relay(j)
         if j == 1:
-            for c in row_sends(tkl, tk_s, tk_r, row, 0):
+            for c in row_sends(pin, tk_s, tk_r, row, 0):
                 c.start()
     wait_recv(dw_ref(zhi_dep), dw_r.at[0], zhi_dev)
     ref = dw_ref(zhi_dep)
     dw_c = remote(ref, ref, dw_s.at[2], dw_r.at[2], core_dev)
     dw_c.start()
-    for j in range(2):
+    for j in range(NC):
         for c in wg_send(j):
             c.start()
     wait_recv(dw_ref(core_dep), dw_r.at[1], core_dev)
@@ -286,6 +292,10 @@
             ggu[o, 0:CH] = (h * u * s * (1.0 + g * (1.0 - s))).astype(BF)
             ggu[o, CH : 2 * CH] = (h * w).astype(BF)
 
+        @pl.when(j == NC - 1)
+        def _():
+            grad_in_last(j)
+
         for c in range(4):
             act[:, c * 256 : (c + 1) * 256] = ac[c * 256 : (c + 1) * 256, :].T
 
@@ -307,22 +317,70 @@
             opart[h, :, 0 : 2 * CH] = a
             opart[h, :, 2 * CH : 3 * CH] = b
 
-    def gi_copy(d):
-        r = (row + d) % 8
-        return remote(
-            pin.at[rows(r, 128)], gr.at[row], gi_s.at[d], gi_m.at[row], (dep, r, y)
-        )
-
-    def stage_e2(j):
-        wait_recv(wg_ref(j, zhi_dep), wg_r.at[j, 0], zhi_dev)
-        wg_fwd(j).start()
+    xp, xm, xo = (x + 1) % 4, (x + 3) % 4, (x + 2) % 4
+
+    def half(q, t, n):
+        return pl.ds(pl.multiple_of((q * 2 + t) * 128 + n * 64, 64), 64)
+
+    def gi_copy(t, i):
+        src, dst, dev = (
+            (half(xo, t, 0), g1.at[t, 0], x_dev[0]),
+            (half(xo, t, 1), g1.at[t, 1], x_dev[1]),
+            (half(xp, t, 1), g2.at[t, 0, 1], x_dev[0]),
+            (half(xm, t, 0), g2.at[t, 1, 0], x_dev[1]),
+            (half(xp, t, 0), g2.at[t, 0, 0], x_dev[0]),
+            (half(xm, t, 1), g2.at[t, 1, 1], x_dev[1]),
+        )[i]
+        return remote(pin.at[src], dst, gi_s.at[t, i], gi_m.at[t, i], dev)
+
+    def gi_relay(t):
+        gi_copy(t, 0).wait_recv()
+        pin[half(xp, t, 0)] = (acc[half(xp, t, 0)] + g1[t, 0].astype(F32)).astype(BF)
+        gi_copy(t, 4).start()
+        gi_copy(t, 1).wait_recv()
+        pin[half(xm, t, 1)] = (acc[half(xm, t, 1)] + g1[t, 1].astype(F32)).astype(BF)
+        gi_copy(t, 5).start()
+
+    def gi_sum(t):
+        for i in (2, 3, 4, 5):
+            gi_copy(t, i).wait_recv()
+        o = rows(x * 2 + t, 128)
+        first = g2[t, 0].astype(F32) + g2[t, 1].astype(F32)
+        return acc[o, :] + first.reshape(128, 1024)
+
+    gz_copy = remote(gs, gz, gz_s, gz_m, zlo_dev)
+
+    def wait_weights(j):
         wait_recv(wg_ref(j, core_dep), wg_r.at[j, 1], core_dev)
         wait_recv(wg_ref(j, (1 - zh) * 2 + (1 - co)), wg_r.at[j, 2], core_dev)
+
+    def stage_e2(j):
+        wait_weights(j)
 
         @pl.loop(0, 4)
         def _(q):
             o = rows(q, 256)
             acc[o, :] += dot_nt(ggu[o, :], wgu[j])
+
+    def grad_in_last(j):
+        wait_weights(j)
+
+        def part(q):
+            o = rows(q, 256)
+            t = acc[o, :] + dot_nt(ggu[o, :], wgu[j])
+            acc[o, :] = t
+            pin[o, :] = t.astype(BF)
+
+        part(xo)
+        for i in (0, 1):
+            gi_copy(1 - zl, i).start()
+        part(xp)
+        gi_copy(1 - zl, 2).start()
+        part(xm)
+        gi_copy(1 - zl, 3).start()
+        for i in (0, 1, 2, 3):
+            gi_copy(zl, i).start()
+        part(x)
 
     def stage_f(j):
         @pl.when(j >= 2)
@@ -354,22 +412,22 @@
         def _():
             stage_c(k - 1)
 
-        @when((k >= AHEAD - 2) & (k + 2 < NC))
-        def _():
-            for c in gp_step1(k + 2):
+        @when((k >= AHEAD) & (k < NC))
+        def _():
+            for c in gp_step1(k):
                 c.start()
 
-        @when(k + 2 < NC)
-        def _():
-            for c in wg_send(k + 2):
+        @when((k >= 1) & (k < NC + 1))
+        def _():
+            wait_recv(wg_ref(k - 1, zhi_dep), wg_r.at[k - 1, 0], zhi_dev)
+            wg_fwd(k - 1).start()
+
+        @when(k == 0)
+        def _():
+            wait_recv(pin.at[rows(zlo_row, 128)], tk_r.at[zlo_row], zlo_dev)
+            for c in row_sends(pin, tk_s, tk_r, zlo_row, 1):
                 c.start()
 
-        @when(k == 0)
-        def _():
-            wait_recv(tkl.at[rows(zlo_row, 128)], tk_r.at[zlo_row], zlo_dev)
-            for c in row_sends(tkl, tk_s, tk_r, zlo_row, 1):
-                c.start()
-
         @when((k >= 3) & (k < NC + 3))
         def _():
             stage_f(k - 3)
@@ -386,60 +444,56 @@
         def _():
             stage_d(k - 1)
 
-        @when((k >= AHEAD - 2) & (k + 2 < NC))
-        def _():
-            gp_relay(k + 2)
+        @when((k >= AHEAD) & (k < NC))
+        def _():
+            gp_relay(k)
 
         @when(k == 1)
         def _():
             for i in range(3):
-                wait_recv(tkl.at[rows(xs[i], 128)], tk_r.at[xs[i]], x_dev[i])
+                wait_recv(pin.at[rows(xs[i], 128)], tk_r.at[xs[i]], x_dev[i])
             for d in (1, 3, 2):
                 r = ((x + d) % 4) * 2 + (1 - zl)
-                wait_recv(tkl.at[rows(r, 128)], tk_r.at[r], zlo_dev)
-            cp = pltpu.make_async_copy(tkl, pin, loc.at[3])
-            cp.start()
-            cp.wait()
+                wait_recv(pin.at[rows(r, 128)], tk_r.at[r], zlo_dev)
+            for c in row_sends(pin, tk_s, tk_r, row, 0) + row_sends(pin, tk_s, tk_r, zlo_row, 1):
+                c.wait_send()
 
             @pl.loop(0, 4)
             def _(q):
                 o = rows(q, 256)
                 tkt[:, o] = pin[o, :].T
 
-        @when((k >= 2) & (k < NC + 2))
+        @when((k >= 2) & (k < NC + 1))
         def _():
             stage_e2(k - 2)
 
-        @when(k == NC + 1)
-        def _():
-            pin[...] = acc[...].astype(BF)
-            for d in (4, 3, 5, 2, 6, 1, 7):
-                gi_copy(d).start()
-
         @when(k >= 4)
         def _():
             stage_g(k - 4)
 
         return carry
 
-    lax.fori_loop(0, NC + 4, body, 0)
-
-    total = acc[rows(row, 128), :]
-    for d in (1, 7, 2, 6, 3, 5, 4):
-        r = (row + d) % 8
-        wait_recv(gr.at[r], gi_m.at[r], (dep, r, y))
-        total = total + gr[r].astype(F32)
-    gin_out[...] = total.astype(BF)
+    lax.fori_loop(0, NC + 2, body, 0)
+    gi_relay(1 - zl)
+    stage_f(NC - 1)
+    gi_relay(zl)
+    stage_g(NC - 2)
+    gs[...] = gi_sum(1 - zl).astype(BF)
+    gz_copy.start()
+    stage_g(NC - 1)
+    total = gi_sum(zl)
+    gz_copy.wait_recv()
+    gin_out[...] = (total + gz[...].astype(F32)).astype(BF)
 
     for c in row_sends(go, go_s, go_r, row, 0) + row_sends(go, go_s, go_r, zlo_row, 1):
-        c.wait_send()
-    for c in row_sends(tkl, tk_s, tk_r, row, 0) + row_sends(tkl, tk_s, tk_r, zlo_row, 1):
         c.wait_send()
     dw_a.wait_send()
     dw_b.wait_send()
     dw_c.wait_send()
-    for d in range(1, 8):
-        gi_copy(d).wait_send()
+    for t in range(2):
+        for i in range(6):
+            gi_copy(t, i).wait_send()
+    gz_copy.wait_send()
 
     def drain(j, carry):
         for c in (*gp_step1(j), *gp_step2(j), *wg_send(j), wg_fwd(j), *rs1_copies(j)):
@@ -455,6 +509,15 @@
         return carry
 
     lax.fori_loop(0, NC, drain, 0)
+
+
+def copy_kernel(a0, a1, a2, a3, b0, b1, b2, b3, sem):
+    pairs = ((a0, b0), (a1, b1), (a2, b2), (a3, b3))
+    copies = [pltpu.make_async_copy(a, b, sem.at[i]) for i, (a, b) in enumerate(pairs)]
+    for c in copies:
+        c.start()
+    for c in copies:
+        c.wait()
 
 
 def shards(tokens_in, grad_out, gate_pre, up_pre, gate_weight, up_weight, down_weight):
@@ -470,10 +533,9 @@
             jax.ShapeDtypeStruct((256, 1792), BF),
             jax.ShapeDtypeStruct((256, 1792), BF),
             jax.ShapeDtypeStruct((1792, 256), BF),
-            jax.ShapeDtypeStruct((1024, 1024), BF),
         ],
         in_specs=[hbm] * 7,
-        out_specs=[vmem] * 4 + [hbm],
+        out_specs=[vmem] * 4,
         scratch_shapes=[
             vm((1024, 1024), BF),
             vm((1024, 1024), BF),
@@ -492,7 +554,10 @@
             vm((CH, 1024), BF),
             vm((1024, 1024), F32),
             vm((1024, 1024), BF),
-            vm((8, 128, 1024), BF),
+            vm((2, 2, 64, 1024), BF),
+            vm((2, 2, 2, 64, 1024), BF),
+            vm((128, 1024), BF),
+            vm((128, 1024), BF),
             vm((2, 2, 256, 3 * CH), BF),
             vm((NC, 2, 256, 3 * CH), BF),
             vm((2, 256, 3 * CH), F32),
@@ -511,7 +576,8 @@
             dma((NC, 2)), dma((NC, 2)),
             dma((NC,)), dma((NC,)),
             dma((NC,)), dma((NC,)),
-            dma((8,)), dma((8,)),
+            dma((2, 6)), dma((2, 6)),
+            dma, dma,
         ],
         compiler_params=pltpu.CompilerParams(
             collective_id=0, has_side_effects=True, vmem_limit_bytes=62 * 2**20
@@ -521,7 +587,16 @@
         ),
         name="swiglu_backward",
     )(tokens_in, grad_out, gate_pre, up_pre, gate_weight, up_weight, down_weight)
-    return tuple(outs[:4])
+    return tuple(
+        pl.pallas_call(
+            copy_kernel,
+            out_shape=[jax.ShapeDtypeStruct(o.shape, o.dtype) for o in outs],
+            in_specs=[hbm] * 4,
+            out_specs=[vmem] * 4,
+            scratch_shapes=[dma((4,))],
+            name="write_outputs",
+        )(*outs)
+    )
 
 
 def solution(mesh):

time: 197 us -> 166 us (0.84); the launches traced: 194 us -> 165 us
  Pallas kernels: 187 us -> 165 us
  local copies, waits for them, and re-layouts: 5.81 us -> 0 us
    pallas_call x1, Pallas kernels: 187 us -> 161 us  [shards(): pl.pallas_call(functools.partial(kernel, scale), out_shape=[jax.ShapeDtyp...]
    unnamed x8 -> x0, local copies, waits for them, and re-layouts: 5.81 us -> none
    pallas_call x0 -> x1, Pallas kernels: none -> 3.47 us  [shards(): pl.pallas_call(copy_kernel, out_shape=[jax.ShapeDtypeStruct(o.shape, o.dt...]
where the time goes in v2:
time: 166 us; the launch traced here: 165 us
  Pallas kernels  165 us (99%)
    pallas_call x1, Pallas kernels, shards(): pl.pallas_call(functools.partial(kernel, scale), out_shape=[jax.ShapeDtyp...  161 us
    pallas_call x1, Pallas kernels, shards(): pl.pallas_call(copy_kernel, out_shape=[jax.ShapeDtypeStruct(o.shape, o.dt...  3.47 us

profile of v2, /device:TPU:32, one launch (start us, length us, event | category | flops | bytes accessed | tf_op | source)
XLA Modules:
  0.0 165.4 jit_solution(10866306124142995470)
XLA Ops:
  0.6 161.3 %swiglu_backward.1 = (bf16[128,1024]{1,0:T(8,128)(2,1)}, bf16[256,1792]{1,0:T(8,128)(2,1)}, bf16[256,1792]{1,0:T(8,128)(2,1)}, bf16[1792,256]{1,0:T(8,128)(2,1)}) custom-call(bf16[128,1024]{1,0:T(8,128)(2,1)} %tok_in.1, bf16[128,1024]{1,0:T(8,128)(2,1)} %go_in.1, bf16[256,1792]{1,0:T(8,128)(2,1)} %gp_in.1, bf16[256,1792]{1,0:T(8,128)(2,1)} %up_in.1, ...), custom_call_target="tpu_custom_call" | custom-call | flops 22499999744 | bytes 20000000 | tf_op jit(solution)/shard_map/swiglu_backward/pallas_call | solution.py:529
  161.9 3.5 %write_outputs.1 = (bf16[128,1024]{1,0:T(8,128)(2,1)}, bf16[256,1792]{1,0:T(8,128)(2,1)}, bf16[256,1792]{1,0:T(8,128)(2,1)}, bf16[1792,256]{1,0:T(8,128)(2,1)}) custom-call(bf16[128,1024]{1,0:T(8,128)(2,1)} %get-tuple-element.8.a0, bf16[256,1792]{1,0:T(8,128)(2,1)} %get-tuple-element.9.a1, bf16[256,1792]{1,0:T(8,128)(2,1)} %get-tuple-element.10.a2, ...), custom_call_target="tpu_custom_call" | custom-call | tf_op jit(solution)/shard_map/write_outputs/pallas_call | solution.py:591

commit v3 on v2

--- a/solution.py
+++ b/solution.py
@@ -22,6 +22,10 @@
 
 def dot_nn(a, b):
     return lax.dot_general(a, b, (((1,), (0,)), ((), ())), preferred_element_type=F32)
+
+
+def sigmoid(g):
+    return 0.5 * jnp.tanh(0.5 * g) + 0.5
 
 
 def remote(src, dst, ssem, rsem, dev):
@@ -286,16 +290,17 @@
             h = hid[j, c, r, :].astype(F32)
             g = gpu[j, c, 0, r, :].astype(F32)
             u = gpu[j, c, 1, r, :].astype(F32)
-            s = jax.nn.sigmoid(g)
+            s = sigmoid(g)
             w = g * s
             ac[o, :] = (w * u).astype(BF)
-            ggu[o, 0:CH] = (h * u * s * (1.0 + g * (1.0 - s))).astype(BF)
+            ggu[o, 0:CH] = (h * u * (s + w * (1.0 - s))).astype(BF)
             ggu[o, CH : 2 * CH] = (h * w).astype(BF)
 
         @pl.when(j == NC - 1)
         def _():
             grad_in_last(j)
 
+    def stage_e3(j):
         for c in range(4):
             act[:, c * 256 : (c + 1) * 256] = ac[c * 256 : (c + 1) * 256, :].T
 
@@ -439,6 +444,10 @@
         @when(k < NC)
         def _():
             stage_b(k)
+
+        @when((k >= 2) & (k < NC + 2))
+        def _():
+            stage_e3(k - 2)
 
         @when((k >= 1) & (k < NC + 1))
         def _():

time: 166 us -> 164 us (0.988)
  Pallas kernels: 165 us -> 163 us
    pallas_call x1, Pallas kernels: 161 us -> 159 us  [shards(): pl.pallas_call(functools.partial(kernel, scale), out_shape=[jax.ShapeDtyp...]
where the time goes in v3:
time: 164 us
  Pallas kernels  163 us (99%)
    pallas_call x1, Pallas kernels, shards(): pl.pallas_call(functools.partial(kernel, scale), out_shape=[jax.ShapeDtyp...  159 us
    pallas_call x1, Pallas kernels, shards(): pl.pallas_call(copy_kernel, out_shape=[jax.ShapeDtypeStruct(o.shape, o.dt...  3.47 us

profile of v3, /device:TPU:32, one launch (start us, length us, event | category | flops | bytes accessed | tf_op | source)
XLA Modules:
  0.0 163.6 jit_solution(4196778495209729779)
XLA Ops:
  0.6 159.5 %swiglu_backward.1 = (bf16[128,1024]{1,0:T(8,128)(2,1)}, bf16[256,1792]{1,0:T(8,128)(2,1)}, bf16[256,1792]{1,0:T(8,128)(2,1)}, bf16[1792,256]{1,0:T(8,128)(2,1)}) custom-call(bf16[128,1024]{1,0:T(8,128)(2,1)} %tok_in.1, bf16[128,1024]{1,0:T(8,128)(2,1)} %go_in.1, bf16[256,1792]{1,0:T(8,128)(2,1)} %gp_in.1, bf16[256,1792]{1,0:T(8,128)(2,1)} %up_in.1, ...), custom_call_target="tpu_custom_call" | custom-call | flops 22499999744 | bytes 20000000 | tf_op jit(solution)/shard_map/swiglu_backward/pallas_call | solution.py:538
  160.1 3.5 %write_outputs.1 = (bf16[128,1024]{1,0:T(8,128)(2,1)}, bf16[256,1792]{1,0:T(8,128)(2,1)}, bf16[256,1792]{1,0:T(8,128)(2,1)}, bf16[1792,256]{1,0:T(8,128)(2,1)}) custom-call(bf16[128,1024]{1,0:T(8,128)(2,1)} %get-tuple-element.8.a0, bf16[256,1792]{1,0:T(8,128)(2,1)} %get-tuple-element.9.a1, bf16[256,1792]{1,0:T(8,128)(2,1)} %get-tuple-element.10.a2, ...), custom_call_target="tpu_custom_call" | custom-call | tf_op jit(solution)/shard_map/write_outputs/pallas_call | solution.py:600

commit v4 on v3

--- a/solution.py
+++ b/solution.py
@@ -13,7 +13,9 @@
 F32 = jnp.float32
 NC = 7
 CH = 256
-AHEAD = 4
+AHEAD, PASSED = 4, 4
+SEND_AT = {4: 2, 5: 4, 6: 5}
+PASS_AT = {4: 3, 5: 5, 6: 6}
 
 
 def dot_nt(a, b):
@@ -38,10 +40,11 @@
     scale,
     tok_in, go_in, gp_in, up_in, gw_in, uw_in, dw_in,
     gin_out, ggw_out, guw_out, gdw_out,
-    go, tkt, dw, wgu, gpu, rs1s, rs1r, rs2s, rs2r, nb, own, hid, ggu, ac, act, acc, pin, g1, g2, gs, gz,
+    gin_v, ggw_v, guw_v, gdw_v,
+    go, tkt, dw, wgu, gpu, rs1s, rs1r, rs2s, rs2r, nb, own, hid, ggu, ac, got, acc, pin, g1, g2, gs, gz,
     cs, cr, opart, zs, zr, oq,
     loc, go_s, go_r, tk_s, tk_r, dw_s, dw_r, wg_s, wg_r, gp_s, gp_r,
-    rs1_s, rs1_m, rs2_s, rs2_m, ag1_s, ag1_m, ag2_s, ag2_m, c_s, c_m, z_s, z_m, gi_s, gi_m, gz_s, gz_m,
+    rs1_s, rs1_m, rs2_s, rs2_m, ag1_s, ag1_m, ag2_s, ag2_m, c_s, c_m, z_s, z_m, gi_s, gi_m, gz_s, gz_m, out_s,
 ):
     dep = lax.axis_index("depth")
     row = lax.axis_index("row")
@@ -59,6 +62,7 @@
     zlo_dev = (dep, zlo_row, y)
     xs = [((x + d) % 4) * 2 + zl for d in (1, 3, 2)]
     x_dev = [(dep, r, y) for r in xs]
+    xp, xm, xo = (x + 1) % 4, (x + 3) % 4, (x + 2) % 4
 
     def wait_recv(ref, sem, dev):
         remote(ref, ref, sem, sem, dev).wait_recv()
@@ -109,6 +113,53 @@
         pl.semaphore_signal(barrier, inc=1, device_id=dev, device_id_type=MESH)
     pl.semaphore_wait(barrier, len(peers))
 
+    def block(q, t):
+        return pl.ds(pl.multiple_of((q * 2 + t) * 128, 128), 128)
+
+    def half(q, t, n):
+        return pl.ds(pl.multiple_of((q * 2 + t) * 128 + n * 64, 64), 64)
+
+    zo = 1 - zl
+
+    def row_copy(buf, sems, i):
+        o, dev = (
+            (block(x, zl), x_dev[0]),
+            (block(x, zl), x_dev[1]),
+            (block(x, zl), zlo_dev),
+            (block(x, zo), x_dev[0]),
+            (block(x, zo), x_dev[1]),
+            (half(xm, zl, 0), x_dev[0]),
+            (half(xp, zl, 1), x_dev[1]),
+            (half(xm, zo, 0), x_dev[0]),
+            (half(xp, zo, 1), x_dev[1]),
+        )[i]
+        return remote(buf.at[o], buf.at[o], sems[0].at[i], sems[1].at[i], dev)
+
+    def row_start(buf, sems, *steps):
+        for i in steps:
+            row_copy(buf, sems, i).start()
+
+    def row_wait(buf, sems, *steps):
+        for i in steps:
+            o = (
+                block(xm, zl),
+                block(xp, zl),
+                block(x, zo),
+                block(xm, zo),
+                block(xp, zo),
+                half(xo, zl, 0),
+                half(xo, zl, 1),
+                half(xo, zo, 0),
+                half(xo, zo, 1),
+            )[i]
+            wait_recv(buf.at[o], sems[1].at[i], zlo_dev)
+
+    def row_sent(buf, sems):
+        for i in range(9):
+            row_copy(buf, sems, i).wait_send()
+
+    go_sem = (go_s, go_r)
+
     def row_sends(buf, ssem, rsem, r, which):
         ref = buf.at[rows(r, 128)]
         cps = [remote(ref, ref, ssem.at[which, i], rsem.at[r], x_dev[i]) for i in range(3)]
@@ -155,8 +206,7 @@
         return remote(ref, ref, wg_s.at[j, 2], wg_r.at[j, 2], core_dev)
 
     l_go.wait()
-    for c in row_sends(go, go_s, go_r, row, 0):
-        c.start()
+    row_start(go, go_sem, 2, 0, 1)
     for c in l_gp(0):
         c.wait()
     for c in gp_step1(0):
@@ -173,19 +223,26 @@
         if j < AHEAD:
             for c in gp_step1(j):
                 c.start()
-    wait_recv(go.at[rows(zlo_row, 128)], go_r.at[zlo_row], zlo_dev)
-    for c in row_sends(go, go_s, go_r, zlo_row, 1):
-        c.start()
+    row_wait(go, go_sem, 2)
+    row_start(go, go_sem, 3, 4)
+    row_wait(go, go_sem, 0)
+    row_start(go, go_sem, 5)
+    row_wait(go, go_sem, 1)
+    row_start(go, go_sem, 6)
     for j in range(NC):
         for c in l_wg(j):
             c.wait()
     l_tk.wait()
     acc[...] = jnp.zeros_like(acc)
-    for j in range(AHEAD):
+    gp_relay(0)
+    row_wait(go, go_sem, 3)
+    row_start(go, go_sem, 7)
+    row_wait(go, go_sem, 4)
+    row_start(go, go_sem, 8)
+    for c in row_sends(pin, tk_s, tk_r, row, 0):
+        c.start()
+    for j in range(1, PASSED):
         gp_relay(j)
-        if j == 1:
-            for c in row_sends(pin, tk_s, tk_r, row, 0):
-                c.start()
     wait_recv(dw_ref(zhi_dep), dw_r.at[0], zhi_dev)
     ref = dw_ref(zhi_dep)
     dw_c = remote(ref, ref, dw_s.at[2], dw_r.at[2], core_dev)
@@ -194,11 +251,7 @@
         for c in wg_send(j):
             c.start()
     wait_recv(dw_ref(core_dep), dw_r.at[1], core_dev)
-    for i in range(3):
-        wait_recv(go.at[rows(xs[i], 128)], go_r.at[xs[i]], x_dev[i])
-    for d in (1, 3, 2):
-        r = ((x + d) % 4) * 2 + (1 - zl)
-        wait_recv(go.at[rows(r, 128)], go_r.at[r], zlo_dev)
+    row_wait(go, go_sem, 5, 6, 7, 8)
     wait_recv(dw_ref((1 - zh) * 2 + (1 - co)), dw_r.at[2], core_dev)
 
     def rs1_copies(k):
@@ -271,10 +324,10 @@
     def z_copy(j):
         return remote(zs.at[j % 2], zr.at[j], z_s.at[j], z_m.at[j], zhi_dev)
 
-    def grad_parts(p):
-        a = dot_nn(tkt[rows(p, 256), :], ggu[...])
-        b = dot_nn(act[...], go[:, rows(p, 256)])
-        return a, b
+    def grad_parts(c):
+        a = dot_nn(tkt[:, c].reshape(512, 1024), ggu[...])
+        b = dot_nn(got[:, c].reshape(512, 1024), ac[...])
+        return a.reshape(2, 256, 2 * CH), b.reshape(2, 256, CH)
 
     def stage_e1(j):
         wait_recv(gpu.at[j, yo, 0], gp_r.at[j, 2], dn_dev)
@@ -301,31 +354,17 @@
             grad_in_last(j)
 
     def stage_e3(j):
-        for c in range(4):
-            act[:, c * 256 : (c + 1) * 256] = ac[c * 256 : (c + 1) * 256, :].T
-
         @pl.when(j >= 2)
         def _():
             core_copy(j - 2).wait_send()
 
-        @pl.loop(0, 2)
-        def _(h):
-            a, b = grad_parts(h * 2 + (1 - co))
-            cs[j % 2, h, :, 0 : 2 * CH] = a.astype(BF)
-            cs[j % 2, h, :, 2 * CH : 3 * CH] = b.astype(BF)
-
+        a, b = grad_parts(1 - co)
+        cs[j % 2, :, :, 0 : 2 * CH] = a.astype(BF)
+        cs[j % 2, :, :, 2 * CH : 3 * CH] = b.astype(BF)
         core_copy(j).start()
-
-        @pl.loop(0, 2)
-        def _(h):
-            a, b = grad_parts(h * 2 + co)
-            opart[h, :, 0 : 2 * CH] = a
-            opart[h, :, 2 * CH : 3 * CH] = b
-
-    xp, xm, xo = (x + 1) % 4, (x + 3) % 4, (x + 2) % 4
-
-    def half(q, t, n):
-        return pl.ds(pl.multiple_of((q * 2 + t) * 128 + n * 64, 64), 64)
+        a, b = grad_parts(co)
+        opart[:, :, 0 : 2 * CH] = a
+        opart[:, :, 2 * CH : 3 * CH] = b
 
     def gi_copy(t, i):
         src, dst, dev = (
@@ -363,9 +402,8 @@
         wait_weights(j)
 
         @pl.loop(0, 4)
-        def _(q):
-            o = rows(q, 256)
-            acc[o, :] += dot_nt(ggu[o, :], wgu[j])
+        def _(p):
+            acc[:, rows(p, 256)] += dot_nt(ggu[...], wgu[j, rows(p, 256)])
 
     def grad_in_last(j):
         wait_weights(j)
@@ -383,7 +421,7 @@
         gi_copy(1 - zl, 2).start()
         part(xm)
         gi_copy(1 - zl, 3).start()
-        for i in (0, 1, 2, 3):
+        for i in (0, 1):
             gi_copy(zl, i).start()
         part(x)
 
@@ -397,13 +435,23 @@
         z_copy(j).start()
         oq[j % 2] = opart[zh] + cr[j, zh].astype(F32)
 
+    def out_copies(j):
+        c = rows(j, CH)
+        return (
+            pltpu.make_async_copy(ggw_v.at[:, c], ggw_out.at[:, c], out_s.at[j, 0]),
+            pltpu.make_async_copy(guw_v.at[:, c], guw_out.at[:, c], out_s.at[j, 1]),
+            pltpu.make_async_copy(gdw_v.at[c], gdw_out.at[c], out_s.at[j, 2]),
+        )
+
     def stage_g(j):
         wait_recv(zr.at[j], z_m.at[j], zhi_dev)
         t = (oq[j % 2] + zr[j].astype(F32)) * scale
         c = rows(j, CH)
-        ggw_out[:, c] = t[:, 0:CH].astype(BF)
-        guw_out[:, c] = t[:, CH : 2 * CH].astype(BF)
-        gdw_out[c, :] = t[:, 2 * CH : 3 * CH].astype(BF)
+        ggw_v[:, c] = t[:, 0:CH].astype(BF)
+        guw_v[:, c] = t[:, CH : 2 * CH].astype(BF)
+        gdw_v[c, :] = t[:, 2 * CH : 3 * CH].astype(BF).T
+        for copy in out_copies(j):
+            copy.start()
 
     def when(cond):
         return pl.when(cond)
@@ -417,10 +465,12 @@
         def _():
             stage_c(k - 1)
 
-        @when((k >= AHEAD) & (k < NC))
-        def _():
-            for c in gp_step1(k):
-                c.start()
+        for j, step in SEND_AT.items():
+
+            @when(k == step)
+            def _():
+                for c in gp_step1(j):
+                    c.start()
 
         @when((k >= 1) & (k < NC + 1))
         def _():
@@ -445,19 +495,7 @@
         def _():
             stage_b(k)
 
-        @when((k >= 2) & (k < NC + 2))
-        def _():
-            stage_e3(k - 2)
-
-        @when((k >= 1) & (k < NC + 1))
-        def _():
-            stage_d(k - 1)
-
-        @when((k >= AHEAD) & (k < NC))
-        def _():
-            gp_relay(k)
-
-        @when(k == 1)
+        @when(k == 2)
         def _():
             for i in range(3):
                 wait_recv(pin.at[rows(xs[i], 128)], tk_r.at[xs[i]], x_dev[i])
@@ -470,7 +508,22 @@
             @pl.loop(0, 4)
             def _(q):
                 o = rows(q, 256)
-                tkt[:, o] = pin[o, :].T
+                tkt[:, :, :, o] = pin[o, :].T.reshape(2, 2, 256, 256)
+                got[:, :, :, o] = go[o, :].T.reshape(2, 2, 256, 256)
+
+        @when((k >= 2) & (k < NC + 2))
+        def _():
+            stage_e3(k - 2)
+
+        @when((k >= 1) & (k < NC + 1))
+        def _():
+            stage_d(k - 1)
+
+        for j, step in PASS_AT.items():
+
+            @when(k == step)
+            def _():
+                gp_relay(j)
 
         @when((k >= 2) & (k < NC + 1))
         def _():
@@ -484,6 +537,8 @@
 
     lax.fori_loop(0, NC + 2, body, 0)
     gi_relay(1 - zl)
+    for i in (2, 3):
+        gi_copy(zl, i).start()
     stage_f(NC - 1)
     gi_relay(zl)
     stage_g(NC - 2)
@@ -492,10 +547,11 @@
     stage_g(NC - 1)
     total = gi_sum(zl)
     gz_copy.wait_recv()
-    gin_out[...] = (total + gz[...].astype(F32)).astype(BF)
-
-    for c in row_sends(go, go_s, go_r, row, 0) + row_sends(go, go_s, go_r, zlo_row, 1):
-        c.wait_send()
+    gin_v[...] = (total + gz[...].astype(F32)).astype(BF)
+    gin_copy = pltpu.make_async_copy(gin_v, gin_out, loc.at[3])
+    gin_copy.start()
+
+    row_sent(go, go_sem)
     dw_a.wait_send()
     dw_b.wait_send()
     dw_c.wait_send()
@@ -505,6 +561,8 @@
     gz_copy.wait_send()
 
     def drain(j, carry):
+        for copy in out_copies(j):
+            copy.wait()
         for c in (*gp_step1(j), *gp_step2(j), *wg_send(j), wg_fwd(j), *rs1_copies(j)):
             c.wait_send()
         for c in (*rs2_copies(j), *ag1_copies(j), *ag2_copies(j)):
@@ -518,14 +576,29 @@
         return carry
 
     lax.fori_loop(0, NC, drain, 0)
-
-
-def copy_kernel(a0, a1, a2, a3, b0, b1, b2, b3, sem):
-    pairs = ((a0, b0), (a1, b1), (a2, b2), (a3, b3))
-    copies = [pltpu.make_async_copy(a, b, sem.at[i]) for i, (a, b) in enumerate(pairs)]
-    for c in copies:
+    gin_copy.wait()
+
+
+def copy_kernel(a0, a1, a2, a3, b0, b1, b2, b3, v0, v1, v2, v3, sem):
+    sets = ((a0, v0, b0, 1), (a1, v1, b1, 4), (a2, v2, b2, 4), (a3, v3, b3, 4))
+    pieces = []
+    for a, v, b, n in sets:
+        step = a.shape[0] // n
+        pieces += [(a, v, b, pl.ds(i * step, step)) for i in range(n)]
+    reads = [
+        pltpu.make_async_copy(a.at[o], v.at[o], sem.at[0, i])
+        for i, (a, v, _, o) in enumerate(pieces)
+    ]
+    writes = [
+        pltpu.make_async_copy(v.at[o], b.at[o], sem.at[1, i])
+        for i, (_, v, b, o) in enumerate(pieces)
+    ]
+    for c in reads:
         c.start()
-    for c in copies:
+    for r, w in zip(reads, writes):
+        r.wait()
+        w.start()
+    for c in writes:
         c.wait()
 
 
@@ -544,10 +617,14 @@
             jax.ShapeDtypeStruct((1792, 256), BF),
         ],
         in_specs=[hbm] * 7,
-        out_specs=[vmem] * 4,
+        out_specs=[hbm] * 4,
         scratch_shapes=[
+            vm((128, 1024), BF),
+            vm((256, 1792), BF),
+            vm((256, 1792), BF),
+            vm((1792, 256), BF),
             vm((1024, 1024), BF),
-            vm((1024, 1024), BF),
+            vm((2, 2, 256, 1024), BF),
             vm((1792, 1024), BF),
             vm((NC, 1024, 2 * CH), BF),
             vm((NC, 4, 2, 256, CH), BF),
@@ -560,7 +637,7 @@
             vm((NC, 4, 256, CH), BF),
             vm((1024, 2 * CH), BF),
             vm((1024, CH), BF),
-            vm((CH, 1024), BF),
+            vm((2, 2, 256, 1024), BF),
             vm((1024, 1024), F32),
             vm((1024, 1024), BF),
             vm((2, 2, 64, 1024), BF),
@@ -574,7 +651,7 @@
             vm((NC, 256, 3 * CH), BF),
             vm((2, 256, 3 * CH), F32),
             dma((32,)),
-            dma((2, 4)), dma((8,)),
+            dma((9,)), dma((9,)),
             dma((2, 4)), dma((8,)),
             dma((3,)), dma((3,)),
             dma((NC, 3)), dma((NC, 3)),
@@ -587,6 +664,7 @@
             dma((NC,)), dma((NC,)),
             dma((2, 6)), dma((2, 6)),
             dma, dma,
+            dma((NC, 3)),
         ],
         compiler_params=pltpu.CompilerParams(
             collective_id=0, has_side_effects=True, vmem_limit_bytes=62 * 2**20
@@ -601,8 +679,8 @@
             copy_kernel,
             out_shape=[jax.ShapeDtypeStruct(o.shape, o.dtype) for o in outs],
             in_specs=[hbm] * 4,
-            out_specs=[vmem] * 4,
-            scratch_shapes=[dma((4,))],
+            out_specs=[hbm] * 4,
+            scratch_shapes=[*(vm(o.shape, o.dtype) for o in outs), dma((2, 13))],
             name="write_outputs",
         )(*outs)
     )

time: 164 us -> 161 us (0.982)
  Pallas kernels: 163 us -> 160 us
    pallas_call x1, Pallas kernels: 159 us -> 157 us  [shards(): pl.pallas_call(functools.partial(kernel, scale), out_shape=[jax.ShapeDtyp...]
where the time goes in v4:
time: 161 us
  Pallas kernels  160 us (99%)
    pallas_call x1, Pallas kernels, shards(): pl.pallas_call(functools.partial(kernel, scale), out_shape=[jax.ShapeDtyp...  157 us

profile of v4, /device:TPU:32, one launch (start us, length us, event | category | flops | bytes accessed | tf_op | source)
XLA Modules:
  0.0 160.8 jit_solution(15336012497532628239)
XLA Ops:
  0.6 157.3 %swiglu_backward.1 = (bf16[128,1024]{1,0:T(8,128)(2,1)}, bf16[256,1792]{1,0:T(8,128)(2,1)}, bf16[256,1792]{1,0:T(8,128)(2,1)}, bf16[1792,256]{1,0:T(8,128)(2,1)}) custom-call(bf16[128,1024]{1,0:T(8,128)(2,1)} %tok_in.1, bf16[128,1024]{1,0:T(8,128)(2,1)} %go_in.1, bf16[256,1792]{1,0:T(8,128)(2,1)} %gp_in.1, bf16[256,1792]{1,0:T(8,128)(2,1)} %up_in.1, ...), custom_call_target="tpu_custom_call" | custom-call | flops 22499999744 | bytes 20000000 | tf_op jit(solution)/shard_map/swiglu_backward/pallas_call | solution.py:611
  158.0 2.8 %write_outputs.1 = (bf16[128,1024]{1,0:T(8,128)(2,1)}, bf16[256,1792]{1,0:T(8,128)(2,1)}, bf16[256,1792]{1,0:T(8,128)(2,1)}, bf16[1792,256]{1,0:T(8,128)(2,1)}) custom-call(bf16[128,1024]{1,0:T(8,128)(2,1)} %get-tuple-element.8.a0, bf16[256,1792]{1,0:T(8,128)(2,1)} %get-tuple-element.9.a1, bf16[256,1792]{1,0:T(8,128)(2,1)} %get-tuple-element.10.a2, ...), custom_call_target="tpu_custom_call" | custom-call | tf_op jit(solution)/shard_map/write_outputs/pallas_call | solution.py:678

commit v5 on v4

--- a/solution.py
+++ b/solution.py
@@ -93,9 +93,9 @@
             ),
         )
 
-    l_go.start()
     for c in l_gp(0):
         c.start()
+    l_go.start()
     l_dw.start()
     for j in range(1, NC):
         for c in l_gp(j):
@@ -205,12 +205,12 @@
         ref = wg_ref(j, zhi_dep)
         return remote(ref, ref, wg_s.at[j, 2], wg_r.at[j, 2], core_dev)
 
-    l_go.wait()
-    row_start(go, go_sem, 2, 0, 1)
     for c in l_gp(0):
         c.wait()
     for c in gp_step1(0):
         c.start()
+    l_go.wait()
+    row_start(go, go_sem, 2, 0, 1)
     l_dw.wait()
     ref = dw_ref(dep)
     dw_a = remote(ref, ref, dw_s.at[0], dw_r.at[0], zhi_dev)
@@ -233,7 +233,6 @@
         for c in l_wg(j):
             c.wait()
     l_tk.wait()
-    acc[...] = jnp.zeros_like(acc)
     gp_relay(0)
     row_wait(go, go_sem, 3)
     row_start(go, go_sem, 7)
@@ -401,9 +400,17 @@
     def stage_e2(j):
         wait_weights(j)
 
-        @pl.loop(0, 4)
-        def _(p):
-            acc[:, rows(p, 256)] += dot_nt(ggu[...], wgu[j, rows(p, 256)])
+        @pl.when(j == 0)
+        def _():
+            @pl.loop(0, 4)
+            def _(p):
+                acc[:, rows(p, 256)] = dot_nt(ggu[...], wgu[j, rows(p, 256)])
+
+        @pl.when(j > 0)
+        def _():
+            @pl.loop(0, 4)
+            def _(p):
+                acc[:, rows(p, 256)] += dot_nt(ggu[...], wgu[j, rows(p, 256)])
 
     def grad_in_last(j):
         wait_weights(j)
@@ -483,10 +490,6 @@
             for c in row_sends(pin, tk_s, tk_r, zlo_row, 1):
                 c.start()
 
-        @when((k >= 3) & (k < NC + 3))
-        def _():
-            stage_f(k - 3)
-
         @when((k >= 2) & (k < NC + 2))
         def _():
             stage_e1(k - 2)
@@ -533,14 +536,18 @@
         def _():
             stage_g(k - 4)
 
+        @when((k >= 2) & (k < NC + 1))
+        def _():
+            stage_f(k - 2)
+
         return carry
 
     lax.fori_loop(0, NC + 2, body, 0)
     gi_relay(1 - zl)
     for i in (2, 3):
         gi_copy(zl, i).start()
+    gi_relay(zl)
     stage_f(NC - 1)
-    gi_relay(zl)
     stage_g(NC - 2)
     gs[...] = gi_sum(1 - zl).astype(BF)
     gz_copy.start()

time: 161 us -> 161 us (level)
  no operation moved by 1% of the time
where the time goes in v5:
time: 161 us
  Pallas kernels  160 us (99%)
    pallas_call x1, Pallas kernels, shards(): pl.pallas_call(functools.partial(kernel, scale), out_shape=[jax.ShapeDtyp...  157 us

profile of v5, /device:TPU:32, one launch (start us, length us, event | category | flops | bytes accessed | tf_op | source)
XLA Modules:
  0.0 160.8 jit_solution(2810781046044939780)
XLA Ops:
  0.6 157.3 %swiglu_backward.1 = (bf16[128,1024]{1,0:T(8,128)(2,1)}, bf16[256,1792]{1,0:T(8,128)(2,1)}, bf16[256,1792]{1,0:T(8,128)(2,1)}, bf16[1792,256]{1,0:T(8,128)(2,1)}) custom-call(bf16[128,1024]{1,0:T(8,128)(2,1)} %tok_in.1, bf16[128,1024]{1,0:T(8,128)(2,1)} %go_in.1, bf16[256,1792]{1,0:T(8,128)(2,1)} %gp_in.1, bf16[256,1792]{1,0:T(8,128)(2,1)} %up_in.1, ...), custom_call_target="tpu_custom_call" | custom-call | flops 22499999744 | bytes 20000000 | tf_op jit(solution)/shard_map/swiglu_backward/pallas_call | solution.py:618
  157.9 2.8 %write_outputs.1 = (bf16[128,1024]{1,0:T(8,128)(2,1)}, bf16[256,1792]{1,0:T(8,128)(2,1)}, bf16[256,1792]{1,0:T(8,128)(2,1)}, bf16[1792,256]{1,0:T(8,128)(2,1)}) custom-call(bf16[128,1024]{1,0:T(8,128)(2,1)} %get-tuple-element.8.a0, bf16[256,1792]{1,0:T(8,128)(2,1)} %get-tuple-element.9.a1, bf16[256,1792]{1,0:T(8,128)(2,1)} %get-tuple-element.10.a2, ...), custom_call_target="tpu_custom_call" | custom-call | tf_op jit(solution)/shard_map/write_outputs/pallas_call | solution.py:685
